TPU v7x, 256 devices: a whole 4x4x8 slice. The times are simulated.
256 devices in a mesh: row: 8 (over z), col: 32 (over x, y, core).
Axes of the slice: x: 4, y: 4, z: 8, core: 2. Of those that a mesh axis runs over, the one named last changes fastest.
Arguments:
- tokens: bfloat16 [1024, 8192], P('row', 'col'), may hold values from -6 to 6
- gate_weight: bfloat16 [8192, 16384], P('row', 'col'), may hold values from -0.125 to 0.125
- up_weight: bfloat16 [8192, 16384], P('row', 'col'), may hold values from -0.125 to 0.125
- gate_mask: int32 [128, 256], P('row', 'col'), may hold values from 0 to 1, as said below
- up_mask: int32 [128, 256], P('row', 'col'), may hold values from 0 to 1, as said below
- grad_hidden: bfloat16 [1024, 16384], P('row', 'col'), may hold values from -1.1953125 to 1.1953125
Outputs:
- hidden: bfloat16 [1024, 16384], P('row', 'col')
- grad_input: bfloat16 [1024, 8192], P(None, ('row', 'col'))
- grad_gate: bfloat16 [8192, 16384], P('row', 'col')
- grad_up: bfloat16 [8192, 16384], P('row', 'col')
Inputs may be any that keep to these rules, and one draw needn't show every extreme that they name: `gate_mask`: 1 keeps a block of 64 x 64 weights, 0 drops it. `up_mask`: 1 keeps a block of 64 x 64 weights, 0 drops it.
All inputs are finite; a program needn't handle non-finite values.
Results may differ from a plain program's by a relative error of at most 0.024.
Values may be sent and summed in bfloat16 or wider, within the bound.
A program may use at most 128 MiB of HBM per device.

v0:
```python
import jax
import jax.numpy as jnp
from jax import lax
from jax.sharding import PartitionSpec as P


def expand(mask, block_size):
    rows, cols = mask.shape
    grid = jnp.broadcast_to(mask[:, None, :, None], (rows, block_size, cols, block_size))
    return grid.reshape(rows * block_size, cols * block_size)


def shards(tokens, gate_weight, up_weight, gate_mask, up_mask, grad_hidden):
    block_size = gate_weight.shape[0] // gate_mask.shape[0]
    hidden_width = gate_weight.shape[1]
    gate_keep = expand(gate_mask, block_size) > 0
    up_keep = expand(up_mask, block_size) > 0
    gate_masked = jnp.where(gate_keep, gate_weight, jnp.zeros_like(gate_weight))
    up_masked = jnp.where(up_keep, up_weight, jnp.zeros_like(up_weight))
    local_pair = jnp.concatenate([gate_masked, up_masked], axis=1)
    features = lax.all_gather(tokens, "col", axis=1, tiled=True)
    token_cols = lax.all_to_all(features, "row", split_axis=1, concat_axis=0, tiled=True)
    projected = jnp.dot(
        features,
        lax.all_gather(local_pair, "row", axis=0, tiled=True),
        preferred_element_type=jnp.float32,
    )
    gate_value = projected[:, :hidden_width]
    up_value = projected[:, hidden_width:]
    sigmoid_gate = jax.nn.sigmoid(gate_value)
    activated = gate_value * sigmoid_gate
    hidden = (activated * up_value).astype(jnp.bfloat16)
    upstream = grad_hidden.astype(jnp.float32)
    grad_gate_value = (
        upstream * up_value * sigmoid_gate * (1.0 + gate_value * (1.0 - sigmoid_gate))
    ).astype(jnp.bfloat16)
    grad_up_value = (upstream * activated).astype(jnp.bfloat16)
    paired_grads = jnp.concatenate([grad_gate_value, grad_up_value], axis=1)
    all_grads = lax.all_gather(paired_grads, "row", axis=0, tiled=True)
    partial_input = lax.dot_general(
        all_grads, local_pair, (((1,), (1,)), ((), ())), preferred_element_type=jnp.float32
    )
    rounded = lax.optimization_barrier(partial_input.astype(jnp.bfloat16)).astype(jnp.float32)
    grad_input = lax.psum_scatter(
        rounded.astype(jnp.bfloat16), "col", scatter_dimension=1, tiled=True
    )
    weight_sums = lax.dot_general(
        token_cols, all_grads, (((0,), (0,)), ((), ())), preferred_element_type=jnp.float32
    )
    keep_pair = jnp.concatenate([gate_keep, up_keep], axis=1)
    weight_grads = jnp.where(keep_pair, weight_sums, jnp.zeros_like(weight_sums)).astype(
        jnp.bfloat16
    )
    return (hidden, grad_input, weight_grads[:, :hidden_width], weight_grads[:, hidden_width:])


def solution(mesh):
    return jax.shard_map(
        shards,
        mesh=mesh,
        in_specs=(
            P("row", "col"),
            P("row", "col"),
            P("row", "col"),
            P("row", "col"),
            P("row", "col"),
            P("row", "col"),
        ),
        out_specs=(P("row", "col"), P(None, ("row", "col")), P("row", "col"), P("row", "col")),
        check_vma=False,
    )
```

profile of v0, /device:TPU:1, one launch (start us, length us, event | category | flops | bytes accessed | tf_op | source)
XLA Modules:
  0.0 425.5 jit_solution(972089169699528712)
XLA Ops:
  7.2 0.0 copy-start.6
  7.2 0.0 all-gather.6.cloned.1.call-start
  7.2 1.6 copy.35
  8.8 0.0 all-gather.6.cloned.1.call-update
  8.8 0.0 all-gather.4.cloned.1.call-start
  8.9 0.7 broadcast_compare_fusion.1
  9.6 0.3 broadcast_in_dim.6
  9.9 0.0 copy-start.3
  9.9 3.1 gt.15
  13.1 0.0 copy-done.6
  13.1 0.3 broadcast_in_dim.7
  13.4 3.1 gt.17
  16.5 0.0 copy-done.3
  16.5 0.0 copy-start.4
  16.5 0.5 copy.33
  17.1 0.7 copy-done.4
  17.8 0.5 copy.34
  18.3 1.7 broadcast_select_fusion
  20.0 0.0 copy-start
  20.0 1.0 copy-done
  21.0 1.5 pad_maximum_fusion
  22.4 0.0 copy-start.5
  22.4 0.0 all-gather.4.cloned.1.call-update
  22.5 0.0 all-gather.8.cloned.1.call-start
  22.5 0.8 copy-done.5
  23.3 0.1 copy.36
  23.5 40.8 %all-gather.6.cloned.1.call-done = bf16[128,8192]{0,1:T(8,128)(2,1)} async-done(((bf16[128,256]{0,1:T(8,128)(2,1)}), bf16[128,8192]{0,1:T(8,128)(2,1)}) %all-gather.6.cloned.1.call-update) | async-done | bytes 2097168 | tf_op jit(solution)/shard_map/all_gather | solution.py:21
  64.2 173.4 %all-gather.4.cloned.1.call-done = bf16[8192,1024]{0,1:T(8,128)(2,1)} async-done(((bf16[1024,1024]{0,1:T(8,128)(2,1)}), bf16[8192,1024]{0,1:T(8,128)(2,1)}) %all-gather.4.cloned.1.call-update) | async-done | bytes 16777232 | tf_op jit(solution)/shard_map/all_gather | solution.py:25
  237.7 8.7 %convolution_bitcast_fusion = f32[128,1024]{0,1:T(8,128)S(1)} fusion(bf16[8192,1024]{0,1:T(8,128)(2,1)} %all-gather.4.cloned.1.call-done, bf16[128,8192]{0,1:T(8,128)(2,1)} %all-gather.6.cloned.1.call-done), kind=kOutput, calls=%fused_computation.4 | convolution fusion | flops 2147483648 | bytes 19398656 | tf_op jit(solution)/shard_map/dot_general | solution.py:23
  246.4 0.2 fusion.3
  246.6 0.7 pad_maximum_fusion.1
  247.3 0.0 all-gather.8.cloned.1.call-update
  247.3 4.1 all-to-all-start
  251.4 0.0 reduce-scatter.4.cloned.1.call-start
  251.5 74.6 %all-gather.8.cloned.1.call-done = bf16[1024,1024]{0,1:T(8,128)(2,1)} async-done(((bf16[128,1024]{0,1:T(8,128)(2,1)}), bf16[1024,1024]{0,1:T(8,128)(2,1)}) %all-gather.8.cloned.1.call-update) | async-done | bytes 2097168 | tf_op jit(solution)/shard_map/all_gather | solution.py:39
  326.1 5.6 %convolution_convert_fusion = bf16[1024,1024]{1,0:T(8,128)(2,1)} fusion(bf16[1024,1024]{0,1:T(8,128)(2,1)} %all-gather.8.cloned.1.call-done, bf16[1024,512]{0,1:T(8,128)(2,1)S(1)} %get-tuple-element.25, bf16[1024,512]{0,1:T(8,128)(2,1)} %copy-done), kind=kOutput, calls=%fused_computation.3 | convolution fusion | flops 2152726528 | bytes 6291456 | tf_op jit(solution)/shard_map/dot_general | solution.py:40
  331.7 3.9 copy.42
  335.6 0.0 reduce-scatter.4.cloned.1.call-update
  335.7 0.0 all-to-all-done
  335.7 0.0 copy-start.1
  335.7 0.0 copy-start.2
  335.7 2.6 copy.37
  338.3 0.8 copy.38
  339.1 0.0 copy-done.1
  339.1 0.0 copy-done.2
  339.1 4.5 %fusion = bf16[1024,1024]{0,1:T(8,128)(2,1)S(1)} fusion(pred[1024,512]{0,1:T(32,128)(4,1)S(1)} %copy-done.2, pred[1024,512]{0,1:T(32,128)(4,1)S(1)} %copy-done.1, bf16[1024,1024]{0,1:T(8,128)(2,1)} %all-gather.8.cloned.1.call-done, bf16[1024,1024]{1,0:T(8,128)(2,1)} %bitcast.27), kind=kOutput, calls=%fused_computation.1 | convolution fusion | flops 2150629376 | bytes 7340032 | tf_op jit(solution)/shard_map/dot_general | solution.py:47
  343.6 0.2 fusion.6
  343.8 1.3 copy.40
  345.1 1.3 copy.41
  346.5 72.6 %reduce-scatter.4.cloned.1.call-done = bf16[32,1024]{1,0:T(8,128)(2,1)} async-done(((bf16[1024,1024]{1,0:T(8,128)(2,1)}), bf16[32,1024]{1,0:T(8,128)(2,1)}) %reduce-scatter.4.cloned.1.call-update) | async-done | bytes 65552
  (1 shorter events, 0.0 us)
Async XLA Ops:
  7.2 5.9 %copy-start.6 = (s32[16,8]{0,1:T(8,128)S(1)}, s32[16,8]{0,1:T(8,128)}, u32[]{:S(2)}) copy-start(s32[16,8]{0,1:T(8,128)} %param.10) | copy-start | bytes 1540
  7.2 57.1 %all-gather.6.cloned.1.call-start = ((), (), s32[]{:S(2)}) async-start(), calls=%async_computation.3 | async-start | bytes 2162688 | tf_op jit(solution)/shard_map/all_gather | solution.py:21
  8.8 228.9 %all-gather.4.cloned.1.call-start = ((), (), s32[]{:S(2)}) async-start(), calls=%async_computation.2 | async-start | bytes 18874368 | tf_op jit(solution)/shard_map/all_gather | solution.py:25
  9.9 6.6 %copy-start.3 = (bf16[1024,512]{1,0:T(8,128)(2,1)S(1)}, bf16[1024,512]{1,0:T(8,128)(2,1)}, u32[]{:S(2)}) copy-start(bf16[1024,512]{1,0:T(8,128)(2,1)} %param.7) | copy-start | bytes 3145732
  16.5 1.2 copy-start.4
  20.0 1.0 copy-start
  22.4 0.9 copy-start.5
  22.5 303.7 %all-gather.8.cloned.1.call-start = ((), (), s32[]{:S(2)}) async-start(), calls=%async_computation.4 | async-start | bytes 2359296 | tf_op jit(solution)/shard_map/all_gather | solution.py:39
  247.3 88.3 %all-to-all-start = ((bf16[128,8,1024]{0,2,1:T(8,128)(2,1)}), bf16[128,8,1024]{0,2,1:T(8,128)(2,1)S(1)}, u32[]{:S(2)}, u32[]{:S(2)}) async-start(bf16[128,8,1024]{0,2,1:T(8,128)(2,1)} %bitcast.26), calls=%async_computation | async-start | bytes 4194304 | tf_op jit(solution)/shard_map/all_to_all | solution.py:22
  251.4 167.6 %reduce-scatter.4.cloned.1.call-start = ((), (), s32[]{:S(2)}) async-start(), calls=%async_computation.5 | async-start | bytes 2162688
  335.7 3.4 copy-start.1
  335.7 3.4 copy-start.2
Sparse Core Ops, SparseCore 0:
  11.1 53.0 all-gather.5
  66.0 171.6 all-gather.3
  247.4 78.6 all-gather.7
  335.8 83.1 reduce-scatter.3
where the time goes:
time: 426 us
  waiting for transfers between devices  361 us (85%)
  local copies, waits for them, and re-layouts  22.3 us (5%)
  matrix products  18.8 us (4%)
  between operations  13.9 us (3%)
  other arithmetic  4.76 us (1%)
  starting transfers between devices  4.27 us (1%)
    all_gather x1, waiting for transfers between devices, shards(): lax.all_gather(local_pair, 'row', axis=0, tiled=True)  173 us
    all_gather x1, waiting for transfers between devices, shards(): all_grads = lax.all_gather(paired_grads, 'row', axis=0, tiled=True)  74.6 us
    unnamed x5, waiting for transfers between devices  72.6 us
    all_gather x1, waiting for transfers between devices, shards(): features = lax.all_gather(tokens, 'col', axis=1, tiled=True)  40.8 us
    unnamed x22, local copies, waits for them, and re-layouts  12.6 us
    dot_general x1, matrix products, shards(): jnp.dot(features, lax.all_gather(local_pair, 'row', axis=0, tiled=True),...  8.7 us
  transfers between devices with their start and end apart: 5, of which 4 were waited for; matrix products, arithmetic and copies ran while one was open for 8% of the time, Pallas kernels for 0%

commit v1 on v0

v1 whole, which is shorter than its diff:
```python
import functools

import jax
import jax.numpy as jnp
from jax import lax
from jax.experimental import pallas as pl
from jax.experimental.pallas import tpu as pltpu
from jax.sharding import PartitionSpec as P

MESH = pl.DeviceIdType.MESH
BF16 = jnp.bfloat16
F32 = jnp.float32

NZ = 8
NS = 4
TB = 128
DB = 1024
SW = 256
QW = 256
OFFSET = (0, 1, -1, 2, -2, 3, -3, 4)
GROUPS = ((0, 1), (1, 2), (3, 2), (5, 2), (7, 1))


def slot_of(rel):
    high = rel // 5
    return (1 - high) * (2 * rel - 1) + high * (16 - 2 * rel) + 1 - (rel + 7) // 8


def remote(src, dst, send, recv, device):
    return pltpu.make_async_remote_copy(
        src_ref=src, dst_ref=dst, send_sem=send, recv_sem=recv, device_id=device, device_id_type=MESH
    )


def kernel(
    tokens, wg, wu, mg, mu, gh,
    hidden, git, og, ou,
    wgv, wuv, wp, we, mex, tv, tt, sb, rb, gv, ps, cr, sx, xr, sy, yr,
    lsem, osem, a1s, tr, aus, avs, afs, acs, bs, br, dsm, dr, ecs, ecr, exs, exr, eys, eyr,
):
    z = lax.axis_index("row")
    c = lax.axis_index("col")
    m = c // 2
    k = c % 2
    x, y = m // 4, m % 4
    u = x + k * (y - x)
    v = y + k * (x - y)
    q = c % 4
    plane = c // 4

    def dev(u_, v_):
        x_ = u_ + k * (v_ - u_)
        y_ = v_ + k * (u_ - v_)
        return (z, (x_ * 4 + y_) * 2 + k)

    def tpiece(slot, q_):
        return tv.at[slot, :, pl.ds(pl.multiple_of(q_ * QW, QW), QW)]

    def piece(u_, v_, k_):
        x_ = u_ + k_ * (v_ - u_)
        y_ = v_ + k_ * (u_ - v_)
        m_ = x_ * 4 + y_
        return slot_of((m_ // 2 + 16 - 2 * z) % NZ), 2 * (m_ % 2) + k_

    upd = ((z + 1) % NZ, c)
    down = ((z + NZ - 1) % NZ, c)
    ring = (upd, down)
    other = (z, c + 1 - 2 * k)
    to = (plane, 4 * ((z + plane) % NZ) + q)
    frm = ((plane + NZ - z) % NZ, 4 * z + q)
    self_piece = jnp.logical_and(z == 0, c < 4)

    barrier = pltpu.get_barrier_semaphore()
    for d in range(1, 4):
        for target in (dev((u + d) % 4, v), dev(u, (v + d) % 4)):
            pl.semaphore_signal(barrier, inc=1, device_id=target, device_id_type=MESH)
    for target in (other, upd, down):
        pl.semaphore_signal(barrier, inc=1, device_id=target, device_id_type=MESH)

    @pl.when(jnp.logical_not(self_piece))
    def _():
        pl.semaphore_signal(barrier, inc=1, device_id=frm, device_id_type=MESH)

    load_g = pltpu.make_async_copy(wg, wgv, lsem.at[0])
    load_u = pltpu.make_async_copy(wu, wuv, lsem.at[1])
    load_g.start()
    load_u.start()
    pl.semaphore_wait(barrier, 10 - (1 - (z + 7) // 8) * (1 - (c + 28) // 32))

    s0, q0 = piece(u, v, k)
    d0 = slot_of((z + NZ - plane) % NZ)
    send0 = remote(tokens, tpiece(d0, q), a1s.at[0], tr.at[d0 * 4 + q], to)
    own = remote(tokens, tpiece(s0, q0), a1s.at[0], tr.at[s0 * 4 + q0], to)

    @pl.when(jnp.logical_not(self_piece))
    def _():
        send0.start()

    @pl.when(self_piece)
    def _():
        local = pltpu.make_async_copy(tokens, tpiece(s0, q0), lsem.at[2])
        local.start()
        local.wait()

    lane = lax.broadcasted_iota(jnp.int32, (16, 128), 1) // 64
    for which, mask in enumerate((mg, mu)):
        kept = jnp.where(mask[...] > 0, 1.0, 0.0).astype(F32)
        for s in range(NS):
            kept_wide = jnp.where(lane == 0, kept[:, 2 * s : 2 * s + 1], kept[:, 2 * s + 1 : 2 * s + 2])
            for i in range(16):
                mex[i, :, s * SW + which * 128 : s * SW + which * 128 + 128] = jnp.broadcast_to(
                    kept_wide[i : i + 1], (8, 128)
                )
    load_g.wait()
    load_u.wait()

    @pl.loop(0, 16)
    def _(i):
        rows = pl.ds(pl.multiple_of(i * 64, 64), 64)
        flip = (i % 4) * 4 + i // 4
        for s in range(NS):
            for which, raw in enumerate((wgv, wuv)):
                cols = slice(s * SW + which * 128, s * SW + which * 128 + 128)
                val = raw[rows, s * 128 : s * 128 + 128].astype(F32).reshape(8, 8, 128)
                val = (val * mex[i, :, cols]).reshape(64, 128).astype(BF16)
                wp[rows, cols] = val
                we[0, pl.ds(pl.multiple_of(i * 32, 32), 32), cols] = val[:32]
                we[1, pl.ds(pl.multiple_of(flip * 32, 32), 32), cols] = val[32:]

    def send_piece(su, qu, sem, target):
        remote(tpiece(su, qu), tpiece(su, qu), sem, tr.at[su * 4 + qu], target).start()

    def wait_piece(su, qu):
        remote(tpiece(su, qu), tpiece(su, qu), a1s.at[0], tr.at[su * 4 + qu], other).wait_recv()

    vright, vleft = dev(u, (v + 1) % 4), dev(u, (v + 3) % 4)

    @pl.when(jnp.logical_not(self_piece))
    def _():
        own.wait_recv()

    for d in range(4):
        su, qu = piece((u + d) % 4, v, k)
        if d == 0:
            for e in range(1, 4):
                send_piece(su, qu, aus.at[e - 1], dev((u + e) % 4, v))
        else:
            wait_piece(su, qu)
        send_piece(su, qu, avs.at[0, d], vright)
        send_piece(su, qu, avs.at[1, d], vleft)
        send_piece(su, qu, acs.at[d], other)
    for d in range(4):
        for side, vv, onward in ((0, (v + 3) % 4, vright), (1, (v + 1) % 4, vleft)):
            su, qu = piece((u + d) % 4, vv, k)
            wait_piece(su, qu)
            if (d < 2) == (side == 0):
                send_piece(su, qu, afs.at[d], onward)
            send_piece(su, qu, acs.at[4 + 2 * d + side], other)
    for d in range(4):
        su, qu = piece((u + d) % 4, (v + 2) % 4, k)
        wait_piece(su, qu)
        send_piece(su, qu, acs.at[12 + d], other)
    for d in range(4):
        for e in range(4):
            su, qu = piece(d, e, 1 - k)
            wait_piece(su, qu)

    def transposed(slot, s):
        cols = slice(s * QW, s * QW + QW)
        tt[cols, slot * TB : slot * TB + TB] = tv[slot, :, cols].T

    def scols(s):
        return pl.ds(pl.multiple_of(s * SW, SW), SW)

    def b_copy(d, step, s):
        return remote(sb.at[d, step, s], rb.at[d, step, s], bs.at[d, step, s], br.at[d, step, s], ring[d])

    def partial_sum(slot, count, s):
        rows = tv[slot : slot + count].reshape(count * TB, DB)
        return jnp.dot(rows, wp[:, s * SW : s * SW + SW], preferred_element_type=F32)

    for s in range(NS):
        d = s // 2
        sb[d, 0, s] = partial_sum(7, 1, s).astype(BF16)
        b_copy(d, 0, s).start()
    for step, slot in ((1, 5), (2, 3), (3, 1)):
        for s in range(NS):
            val = partial_sum(slot, 2, s)
            for d in range(2):
                term = val[d * TB : d * TB + TB]
                if step > 1 or s // 2 == d:
                    b_copy(d, step - 1, s).wait_recv()
                    term = term + rb[d, step - 1, s].astype(F32)
                sb[d, step, s] = term.astype(BF16)
                b_copy(d, step, s).start()
            transposed(slot, s)
            transposed(slot + 1, s)

    def d_copy(dst, src, s, d, step):
        cols = slice(s * SW, s * SW + SW)
        return remote(gv.at[src, :, cols], gv.at[dst, :, cols], dsm.at[d, step, s], dr.at[dst, s], ring[d])

    def d_wait(slot, s):
        cols = slice(s * SW, s * SW + SW)
        part = gv.at[slot, :, cols]
        remote(part, part, dsm.at[0, 0, 0], dr.at[slot, s], upd).wait_recv()

    for s in range(NS):
        val = partial_sum(0, 1, s)
        for d in range(2):
            b_copy(d, 3, s).wait_recv()
            val = val + rb[d, 3, s].astype(F32)
        gate, up = val[:, :128], val[:, 128:]
        hcols = slice(s * 128, s * 128 + 128)
        up_grad = gh[:, hcols].astype(F32)
        sig = 1.0 / (1.0 + jnp.exp(-gate))
        act = gate * sig
        hidden[:, hcols] = (act * up).astype(BF16)
        gv[0, :, s * SW : s * SW + 128] = (up_grad * up * sig * (1.0 + gate * (1.0 - sig))).astype(BF16)
        gv[0, :, s * SW + 128 : s * SW + SW] = (up_grad * act).astype(BF16)
        d_copy(2, 0, s, 0, 0).start()
        d_copy(1, 0, s, 1, 0).start()
        transposed(0, s)
        transposed(7, s)

    def grads_of(g):
        first, count = GROUPS[g]
        return gv[first : first + count].reshape(count * TB, DB)

    def half_dot(g, side, i):
        rows = we[side, i * 256 : i * 256 + 256, :]
        out = lax.dot_general(rows, grads_of(g), (((1,), (1,)), ((), ())), preferred_element_type=F32)
        return out.reshape(2, 4, 32, GROUPS[g][1] * TB)

    def wide(ref, g, *index):
        w = GROUPS[g][1] * TB
        rest = len(ref.shape) - 1 - len(index) - 1
        return ref.at[(g,) + index + (slice(None),) * rest + (slice(0, w),)]

    def core_copy(g):
        return remote(wide(ps, g), wide(cr, g), ecs.at[g], ecr.at[g], other)

    def x_copy(g, d):
        return remote(
            wide(sx, g, (u + d) % 4), wide(xr, g, d - 1), exs.at[g, d - 1], exr.at[g, d - 1], dev((u + d) % 4, v)
        )

    def y_copy(g, d):
        return remote(
            wide(sy, g, (v + d) % 4), wide(yr, g, d - 1), eys.at[g, d - 1], eyr.at[g, d - 1], dev(u, (v + d) % 4)
        )

    def e1(g):
        for i in range(2):
            wide(ps, g)[2 * i : 2 * i + 2] = half_dot(g, 1 - k, i).astype(BF16)
        core_copy(g).start()

    def e2(g):
        for i in range(2):
            val = half_dot(g, k, i)
            if i == 0:
                core_copy(g).wait_recv()
            val = val + wide(cr, g)[2 * i : 2 * i + 2].astype(F32)
            wide(sx, g)[2 * i : 2 * i + 2] = val.astype(BF16)
        for d in range(1, 4):
            x_copy(g, d).start()

    def e3(g):
        val = wide(sx, g, u)[...].astype(F32)
        for d in range(1, 4):
            x_copy(g, d).wait_recv()
            val = val + wide(xr, g, d - 1)[...].astype(F32)
        wide(sy, g)[...] = val.astype(BF16)
        for d in range(1, 4):
            y_copy(g, d).start()

    def e4(g):
        first, count = GROUPS[g]
        val = wide(sy, g, v)[...].astype(F32)
        for d in range(1, 4):
            y_copy(g, d).wait_recv()
            val = val + wide(yr, g, d - 1)[...].astype(F32)
        val = val.astype(BF16)
        for j in range(count):
            block = (z + NZ + OFFSET[first + j]) % NZ
            git[:, pl.ds(pl.multiple_of(block * TB, TB), TB)] = val[:, j * TB : j * TB + TB]

    e1(0)
    for step in range(1, 5):
        for s in range(NS):
            if step < 4:
                for d, slot in ((0, 2 * step), (1, 2 * step - 1)):
                    d_wait(slot, s)
                    if step < 3 or s // 2 == d:
                        d_copy(min(slot + 2, 7), slot, s, d, step).start()
            else:
                d_wait(7, s)
            g = step - 1
            if s == 0:
                e2(g)
            elif s == 1 and g > 0:
                e4(g - 1)
            elif s == 2:
                e3(g)
        e1(step)

    def weight_rows(i):
        rows = slice(i * 256, i * 256 + 256)
        for s in range(NS):
            right = gv[:, :, s * SW : s * SW + SW].reshape(NZ * TB, SW)
            val = jnp.dot(tt[rows, :], right, preferred_element_type=F32)
            for b in range(4):
                row = i * 4 + b
                for which, out in enumerate((og, ou)):
                    cols = slice(s * SW + which * 128, s * SW + which * 128 + 128)
                    keep = mex[row, 0:1, cols] > 0.0
                    part = val[b * 64 : b * 64 + 64, which * 128 : which * 128 + 128]
                    out[row * 64 : row * 64 + 64, s * 128 : s * 128 + 128] = jnp.where(keep, part, 0.0).astype(BF16)

    e4(3)
    e2(4)
    weight_rows(0)
    e3(4)
    weight_rows(1)
    e4(4)
    weight_rows(2)
    weight_rows(3)

    @pl.when(jnp.logical_not(self_piece))
    def _():
        send0.wait_send()

    def sent(sem):
        remote(tpiece(0, 0), tpiece(0, 0), sem, tr.at[0], other).wait_send()

    for d in range(3):
        sent(aus.at[d])
    for d in range(4):
        sent(avs.at[0, d])
        sent(avs.at[1, d])
        sent(afs.at[d])
    for d in range(16):
        sent(acs.at[d])
    for d in range(2):
        for s in range(NS):
            if s // 2 == d:
                b_copy(d, 0, s).wait_send()
            for step in range(1, 4):
                b_copy(d, step, s).wait_send()
            for step in range(4):
                if step < 3 or s // 2 == d:
                    d_copy(1, 0, s, d, step).wait_send()
    for g in range(len(GROUPS)):
        core_copy(g).wait_send()
        for d in range(1, 4):
            x_copy(g, d).wait_send()
            y_copy(g, d).wait_send()


def shards(tokens, gate_weight, up_weight, gate_mask, up_mask, grad_hidden):
    vmem = pl.BlockSpec(memory_space=pltpu.VMEM)
    hbm = pl.BlockSpec(memory_space=pl.ANY)
    dma = pltpu.SemaphoreType.DMA
    ng = len(GROUPS)
    hidden, git, og, ou = pl.pallas_call(
        kernel,
        out_shape=(
            jax.ShapeDtypeStruct((TB, 512), BF16),
            jax.ShapeDtypeStruct((32, NZ * TB), BF16),
            jax.ShapeDtypeStruct((DB, 512), BF16),
            jax.ShapeDtypeStruct((DB, 512), BF16),
        ),
        in_specs=[hbm, hbm, hbm, vmem, vmem, vmem],
        out_specs=(vmem, vmem, vmem, vmem),
        scratch_shapes=[
            pltpu.VMEM((DB, 512), BF16),
            pltpu.VMEM((DB, 512), BF16),
            pltpu.VMEM((DB, DB), BF16),
            pltpu.VMEM((2, 512, DB), BF16),
            pltpu.VMEM((16, 8, DB), F32),
            pltpu.VMEM((NZ, TB, DB), BF16),
            pltpu.VMEM((DB, NZ * TB), BF16),
            pltpu.VMEM((2, 4, NS, TB, SW), BF16),
            pltpu.VMEM((2, 4, NS, TB, SW), BF16),
            pltpu.VMEM((NZ, TB, DB), BF16),
            pltpu.VMEM((ng, 4, 4, 32, 256), BF16),
            pltpu.VMEM((ng, 4, 4, 32, 256), BF16),
            pltpu.VMEM((ng, 4, 4, 32, 256), BF16),
            pltpu.VMEM((ng, 3, 4, 32, 256), BF16),
            pltpu.VMEM((ng, 4, 32, 256), BF16),
            pltpu.VMEM((ng, 3, 32, 256), BF16),
            dma((3,)),
            dma((2,)),
            dma((1,)),
            dma((32,)),
            dma((3,)),
            dma((2, 4)),
            dma((4,)),
            dma((16,)),
            dma((2, 4, NS)),
            dma((2, 4, NS)),
            dma((2, 4, NS)),
            dma((NZ, NS)),
            dma((ng,)),
            dma((ng,)),
            dma((ng, 3)),
            dma((ng, 3)),
            dma((ng, 3)),
            dma((ng, 3)),
        ],
        compiler_params=pltpu.CompilerParams(
            collective_id=0, has_side_effects=True, vmem_limit_bytes=48 * 1024 * 1024
        ),
    )(tokens, gate_weight, up_weight, gate_mask, up_mask, grad_hidden)
    return hidden, git.T, og, ou


def solution(mesh):
    return jax.shard_map(
        shards,
        mesh=mesh,
        in_specs=(P("row", "col"),) * 6,
        out_specs=(P("row", "col"), P(None, ("row", "col")), P("row", "col"), P("row", "col")),
        check_vma=False,
    )
```

time: 426 us -> 107 us (0.25)
  waiting for transfers between devices: 361 us -> 0 us
  Pallas kernels: 0 us -> 96.4 us
  matrix products: 18.8 us -> 0 us
  local copies, waits for them, and re-layouts: 22.3 us -> 8.26 us
  between operations: 13.9 us -> 0.65 us
  other arithmetic: 4.76 us -> 0 us
  starting transfers between devices: 4.27 us -> 0 us
    all_gather x3 -> x0, waiting for transfers between devices: 289 us -> none  [the longest x1 173 us: shards(): lax.all_gather(local_pair, 'row', axis=0, tiled=True)]
    pallas_call x0 -> x1, Pallas kernels: none -> 96.4 us  [shards(): pl.pallas_call(kernel, out_shape=(jax.ShapeDtypeStruct((TB, 512), BF16),...]
    unnamed x5 -> x0, waiting for transfers between devices: 72.6 us -> none
    dot_general x3 -> x0, matrix products: 18.8 us -> none  [the longest x1 8.7 us: shards(): jnp.dot(features, lax.all_gather(local_pair, 'row', axis=0, tiled=True),...]
    gt x2 -> x0, local copies, waits for them, and re-layouts: 6.26 us -> none  [the longest x1 3.14 us: shards(): gate_keep = expand(gate_mask, block_size) > 0]
    unnamed x22 -> x16, local copies, waits for them, and re-layouts: 12.6 us -> 8.26 us
  transfers between devices with their start and end apart: 5 -> 0, of which waited for: 4 -> 0; matrix products, arithmetic and copies ran while one was open for 8% -> 0% of each run, Pallas kernels for 0% -> 0%
where the time goes in v1:
time: 107 us; the launch traced here: 105 us
  Pallas kernels  96.4 us (90%)
  local copies, waits for them, and re-layouts  8.26 us (8%)
    pallas_call x1, Pallas kernels, shards(): pl.pallas_call(kernel, out_shape=(jax.ShapeDtypeStruct((TB, 512), BF16),...  96.4 us
    unnamed x16, local copies, waits for them, and re-layouts  8.26 us

profile of v1, /device:TPU:1, one launch (start us, length us, event | category | flops | bytes accessed | tf_op | source)
XLA Modules:
  0.0 105.3 jit_solution(6891226622922263657)
XLA Ops:
  0.6 0.0 copy-start.4
  0.6 0.8 copy.10.mg
  1.4 0.0 copy-done.4
  1.4 0.1 copy.11.mu
  1.5 0.0 copy-start
  1.5 1.2 %copy-done = bf16[1024,512]{1,0:T(8,128)(2,1)S(1)} copy-done((bf16[1024,512]{1,0:T(8,128)(2,1)S(1)}, bf16[1024,512]{1,0:T(8,128)(2,1)}, u32[]{:S(2)}) %copy-start) | copy-done | bytes 1048600
  2.7 0.0 copy-start.1
  2.7 1.2 %copy-done.1 = bf16[1024,512]{1,0:T(8,128)(2,1)S(1)} copy-done((bf16[1024,512]{1,0:T(8,128)(2,1)S(1)}, bf16[1024,512]{1,0:T(8,128)(2,1)}, u32[]{:S(2)}) %copy-start.1) | copy-done | bytes 1048600
  3.9 0.0 copy-start.2
  3.9 0.9 copy-done.2
  4.8 0.0 copy-start.3
  4.8 0.8 copy-done.3
  5.7 96.4 %shard_map.93 = (bf16[128,512]{1,0:T(8,128)(2,1)S(1)}, bf16[32,1024]{1,0:T(8,128)(2,1)S(1)}, bf16[1024,512]{1,0:T(8,128)(2,1)S(1)}, bf16[1024,512]{1,0:T(8,128)(2,1)S(1)}) custom-call(bf16[128,256]{1,0:T(8,128)(2,1)S(1)} %copy-done.3, bf16[1024,512]{1,0:T(8,128)(2,1)S(1)} %copy-done, bf16[1024,512]{1,0:T(8,128)(2,1)S(1)} %copy-done.1, s32[16,8]{1,0:T(8,128)S(1)} %copy.10.mg, ...), custom_call_target="tpu_custom_call" | custom-call | tf_op jit(solution)/shard_map/pallas_call | solution.py:365
  102.1 0.7 copy.16
  102.7 0.6 copy.17
  103.4 1.0 copy.18
  104.3 1.0 copy.19
Async XLA Ops:
  0.6 0.8 copy-start.4
  1.5 1.2 %copy-start = (bf16[1024,512]{1,0:T(8,128)(2,1)S(1)}, bf16[1024,512]{1,0:T(8,128)(2,1)}, u32[]{:S(2)}) copy-start(bf16[1024,512]{1,0:T(8,128)(2,1)} %wg.1) | copy-start | bytes 3145732
  2.7 1.2 %copy-start.1 = (bf16[1024,512]{1,0:T(8,128)(2,1)S(1)}, bf16[1024,512]{1,0:T(8,128)(2,1)}, u32[]{:S(2)}) copy-start(bf16[1024,512]{1,0:T(8,128)(2,1)} %wu.1) | copy-start | bytes 3145732
  3.9 0.9 copy-start.2
  4.8 0.8 copy-start.3

commit v2 on v0

v2 whole, which is shorter than its diff:
```python
import jax
import jax.numpy as jnp
from jax import lax
from jax.experimental import pallas as pl
from jax.experimental.pallas import tpu as pltpu
from jax.sharding import PartitionSpec as P

MESH = pl.DeviceIdType.MESH
BF16 = jnp.bfloat16
F32 = jnp.float32

NZ = 8
NS = 4
TB = 128
DB = 1024
SW = 256
QW = 256
OFFSET = (0, 1, -1, 2, -2, 3, -3, 4)
GROUPS = ((0, 1), (1, 2), (3, 2), (5, 2), (7, 1))
PLACE = ((2, 1), (1, 1), (3, 1), (2, 0), (0, 1), (1, 0), (3, 0), (0, 0))
SLOT_AT = tuple(PLACE.index((i % 4, i // 4)) for i in range(8))
REL = tuple(o % NZ for o in OFFSET)
SLOT_OF = tuple(REL.index(r) for r in range(NZ))


def pick(table, i):
    return sum(t * (1 - ((i - j) * (i - j) + 63) // 64) for j, t in enumerate(table))


def remote(src, dst, send, recv, device):
    return pltpu.make_async_remote_copy(
        src_ref=src, dst_ref=dst, send_sem=send, recv_sem=recv, device_id=device, device_id_type=MESH
    )


def kernel(
    tokens, wg, wu, mg, mu, gh,
    hidden_out, git_out, og_out, ou_out,
    wgv, wuv, ghv, hidden, git, og, ou, wp, we, mex, tv, tt, sb, rb, gv,
    ps1, ps2, cr1, cr2, sx1, sx2, er1, er2,
    lsem, osem, ts, tr, bs, br, dsm, dr, ecs, ecr, exs, exr,
):
    z = lax.axis_index("row")
    c = lax.axis_index("col")
    m = c // 2
    k = c % 2
    x, y = m // 4, m % 4
    u = x + k * (y - x)
    v = y + k * (x - y)
    x0, y0 = z // 2, 2 * (z % 2)
    u0 = x0 + k * (y0 - x0)

    def dev(u_, v_):
        x_ = u_ + k * (v_ - u_)
        y_ = v_ + k * (u_ - v_)
        return (z, (x_ * 4 + y_) * 2 + k)

    def tpiece(slot, q_):
        return tv.at[slot, :, pl.ds(pl.multiple_of(q_ * QW, QW), QW)]

    def piece(u_, v_):
        dx = (u_ + k * (v_ - u_) + 4 - x0) % 4
        dy = (v_ + k * (u_ - v_) + 4 - y0) % 4
        return pick(SLOT_AT, dx + 4 * (dy // 2)), 2 * (dy % 2) + k

    upd = ((z + 1) % NZ, c)
    down = ((z + NZ - 1) % NZ, c)
    ring = (upd, down)
    other = (z, c + 1 - 2 * k)

    plane = c // 4
    slot_there = pick(SLOT_OF, (z + NZ - plane) % NZ)
    to_x = (plane // 2 + pick([p[0] for p in PLACE], slot_there)) % 4
    to_y = (2 * (plane % 2) + 2 * pick([p[1] for p in PLACE], slot_there) + m % 2) % 4
    to = (plane, (to_x * 4 + to_y) * 2 + k)
    s0, q0 = piece(u, v)
    frm = ((z + pick(REL, s0)) % NZ, 4 * z + q0)

    load_g = pltpu.make_async_copy(wg, wgv, lsem.at[0])
    load_u = pltpu.make_async_copy(wu, wuv, lsem.at[1])
    load_h = pltpu.make_async_copy(gh, ghv, lsem.at[2])
    load_g.start()
    load_u.start()
    load_h.start()

    barrier = pltpu.get_barrier_semaphore()
    near = [(z, (((x + d // 4) % 4) * 4 + (y + d % 4) % 4) * 2 + k) for d in range(16)]
    for target in near[1:] + [other, upd, down, frm]:
        pl.semaphore_signal(barrier, inc=1, device_id=target, device_id_type=MESH)
    pl.semaphore_wait(barrier, 19)

    remote(tokens, tpiece(slot_there, c % 4), ts.at[0], tr.at[slot_there * 4 + c % 4], to).start()

    lane = lax.broadcasted_iota(jnp.int32, (16, 128), 1) // 64
    for which, mask in enumerate((mg, mu)):
        kept = jnp.where(mask[...] > 0, 1.0, 0.0).astype(F32).T
        for s in range(NS):
            kept_wide = jnp.where(lane == 0, kept[:, 2 * s : 2 * s + 1], kept[:, 2 * s + 1 : 2 * s + 2])
            for i in range(16):
                mex[i, :, s * SW + which * 128 : s * SW + which * 128 + 128] = jnp.broadcast_to(
                    kept_wide[i : i + 1], (8, 128)
                )
    load_g.wait()
    load_u.wait()
    load_h.wait()

    @pl.loop(0, 16)
    def _(i):
        rows = pl.ds(pl.multiple_of(i * 64, 64), 64)
        half = pl.ds(pl.multiple_of(i * 32, 32), 32)
        for s in range(NS):
            for which, raw in enumerate((wgv, wuv)):
                cols = slice(s * SW + which * 128, s * SW + which * 128 + 128)
                val = raw[rows, s * 128 : s * 128 + 128].astype(F32).reshape(8, 8, 128)
                val = (val * mex[i, :, cols]).reshape(64, 128).astype(BF16)
                wp[rows, cols] = val
                we[0, half, cols] = val[:32]
                we[1, half, cols] = val[32:]

    def send_piece(su, qu, target):
        remote(tpiece(su, qu), tpiece(su, qu), ts.at[0], tr.at[su * 4 + qu], target).start()

    def wait_piece(su, qu):
        remote(tpiece(su, qu), tpiece(su, qu), ts.at[0], tr.at[su * 4 + qu], other).wait_recv()

    wait_piece(s0, q0)
    for d in (1, 3, 2):
        send_piece(s0, q0, dev((u + d) % 4, v))
    for d in (1, 3, 2):
        send_piece(s0, q0, dev(u, (v + d) % 4))
    for off in (0, 1, 3, 2):
        line = (u0 + off) % 4

        @pl.when(line != u)
        def _(line=line):
            su, qu = piece(line, v)
            wait_piece(su, qu)
            for d in (1, 3, 2):
                send_piece(su, qu, dev(u, (v + d) % 4))

    def swap(slot):
        for b in range(2):
            x_ = (x0 + PLACE[slot][0]) % 4
            y_ = (y0 + 2 * PLACE[slot][1] + b) % 4
            q_ = 2 * b + k

            @pl.when(y_ + k * (x_ - y_) != v)
            def _(q_=q_):
                wait_piece(slot, q_)

            send_piece(slot, q_, other)

    def ready(slot):
        for b in range(2):
            wait_piece(slot, 2 * b + 1 - k)

    def transposed(slot, s):
        cols = slice(s * QW, s * QW + QW)
        tt[cols, slot * TB : slot * TB + TB] = tv[slot, :, cols].T

    def b_copy(d, step, s):
        i = s % 2 if step == 0 else 4 * step - 2 + s
        return remote(sb.at[d, i], rb.at[d, i], bs.at[d], br.at[d, i], ring[d])

    def b_in(d, step, s):
        b_copy(d, step, s).wait_recv()
        return rb[d, s % 2 if step == 0 else 4 * step - 2 + s].astype(F32)

    def b_out(d, step, s, val):
        sb[d, s % 2 if step == 0 else 4 * step - 2 + s] = val.astype(BF16)
        b_copy(d, step, s).start()

    def partial_sum(slot, count, s):
        rows = tv[slot : slot + count].reshape(count * TB, DB)
        return jnp.dot(rows, wp[:, s * SW : s * SW + SW], preferred_element_type=F32)

    for slot in (7, 5, 6):
        swap(slot)
    ready(7)
    for s in (0, 2, 1, 3):
        b_out(s // 2, 0, s, partial_sum(7, 1, s))
    for slot in (3, 4):
        swap(slot)
    ready(5)
    ready(6)
    for d, s in ((0, 2), (1, 0), (0, 3), (1, 1)):
        b_out(d, 1, s, partial_sum(5 + d, 1, s))
    for slot in (1, 2, 0):
        swap(slot)
    for s in range(NS):
        transposed(7, s)
    for d, s in ((0, 0), (1, 2), (0, 1), (1, 3)):
        val = partial_sum(5 + d, 1, s)
        b_out(d, 1, s, val + b_in(d, 0, s))
    for step, slot in ((2, 3), (3, 1)):
        ready(slot)
        ready(slot + 1)
        for s in range(NS):
            val = partial_sum(slot, 2, s)
            for d in range(2):
                b_out(d, step, s, val[d * TB : d * TB + TB] + b_in(d, step - 1, s))
            transposed(slot, s)
            transposed(slot + 1, s)
            transposed(slot + 2, s)
            if step == 2:
                transposed(6, s)
    ready(0)

    def d_copy(dst, src, s, d):
        cols = slice(s * SW, s * SW + SW)
        return remote(gv.at[src, :, cols], gv.at[dst, :, cols], dsm.at[d], dr.at[dst, s], ring[d])

    def d_wait(slot, s):
        d_copy(slot, slot, s, 0).wait_recv()

    for s in range(NS):
        val = partial_sum(0, 1, s)
        for d in range(2):
            val = val + b_in(d, 3, s)
        gate, up = val[:, :128], val[:, 128:]
        hcols = slice(s * 128, s * 128 + 128)
        up_grad = ghv[:, hcols].astype(F32)
        sig = 1.0 / (1.0 + jnp.exp(-gate))
        act = gate * sig
        gv[0, :, s * SW : s * SW + 128] = (up_grad * up * sig * (1.0 + gate * (1.0 - sig))).astype(BF16)
        gv[0, :, s * SW + 128 : s * SW + SW] = (up_grad * act).astype(BF16)
        d_copy(2, 0, s, 0).start()
        d_copy(1, 0, s, 1).start()
        hidden[:, hcols] = (act * up).astype(BF16)
        transposed(0, s)
    store_h = pltpu.make_async_copy(hidden, hidden_out, osem.at[0])
    store_h.start()

    def of_group(one, two, g):
        return one.at[g // 4] if GROUPS[g][1] == 1 else two.at[g - 1]

    def core_dot(g, side):
        first, count = GROUPS[g]
        grads = gv[first : first + count].reshape(count * TB, DB)
        out = lax.dot_general(we[side], grads, (((1,), (1,)), ((), ())), preferred_element_type=F32)
        return out.reshape(16, 32, count * TB)

    def core_copy(g):
        return remote(of_group(ps1, ps2, g), of_group(cr1, cr2, g), ecs.at[g], ecr.at[g], other)

    def e1(g):
        of_group(ps1, ps2, g)[...] = core_dot(g, 1 - k).astype(BF16)
        core_copy(g).start()

    def e2(g):
        val = core_dot(g, k)
        core_copy(g).wait_recv()
        sums = of_group(sx1, sx2, g)
        sums[...] = (val + of_group(cr1, cr2, g)[...].astype(F32)).astype(BF16)
        for d in range(1, 16):
            chip = ((x + d // 4) % 4) * 4 + (y + d % 4) % 4
            remote(sums.at[chip], of_group(er1, er2, g).at[d - 1], exs.at[g], exr.at[g], near[d]).start()

    def plane_all(g):
        sums, got = of_group(sx1, sx2, g), of_group(er1, er2, g)
        return remote(sums.at[0:15], got, exs.at[g], exr.at[g], other)

    def e3(g):
        first, count = GROUPS[g]
        plane_all(g).wait_recv()
        val = of_group(sx1, sx2, g)[m].astype(F32)
        for d in range(15):
            val = val + of_group(er1, er2, g)[d].astype(F32)
        val = val.astype(BF16)
        for j in range(count):
            block = (z + NZ + OFFSET[first + j]) % NZ
            git[:, pl.ds(pl.multiple_of(block * TB, TB), TB)] = val[:, j * TB : j * TB + TB]

    for step in range(1, 4):
        for s in range(NS):
            for d, slot in ((0, 2 * step), (1, 2 * step - 1)):
                d_wait(slot, s)
                if step < 3 or s // 2 == d:
                    d_copy(min(slot + 2, 7), slot, s, d).start()
            if s == 0:
                e1(step - 1)
            elif s == 2:
                e2(step - 1)
            elif s == 3 and step > 1:
                e3(step - 2)
    d_wait(7, 0)
    d_wait(7, 2)
    e1(3)
    d_wait(7, 1)
    d_wait(7, 3)
    e1(4)
    e2(3)
    e2(4)

    def store_rows(i):
        rows = slice(i * 256, i * 256 + 256)
        return [
            pltpu.make_async_copy(val.at[rows], out.at[rows], osem.at[2 + 2 * i + j])
            for j, (val, out) in enumerate(((og, og_out), (ou, ou_out)))
        ]

    def weight_rows(i):
        rows = slice(i * 256, i * 256 + 256)
        for s in range(NS):
            right = gv[:, :, s * SW : s * SW + SW].reshape(NZ * TB, SW)
            val = jnp.dot(tt[rows, :], right, preferred_element_type=F32)
            for b in range(4):
                row = i * 4 + b
                for which, out in enumerate((og, ou)):
                    cols = slice(s * SW + which * 128, s * SW + which * 128 + 128)
                    keep = mex[row, 0:1, cols] > 0.0
                    part = val[b * 64 : b * 64 + 64, which * 128 : which * 128 + 128]
                    out[row * 64 : row * 64 + 64, s * 128 : s * 128 + 128] = jnp.where(keep, part, 0.0).astype(BF16)
        for copy in store_rows(i):
            copy.start()

    for i in range(4):
        weight_rows(i)
    e3(2)
    e3(3)
    e3(4)
    store_i = pltpu.make_async_copy(git, git_out, osem.at[1])
    store_i.start()

    remote(tv, tv, ts.at[0], tr.at[0], other).wait_send()
    for d in range(2):
        remote(sb.at[d], sb.at[d], bs.at[d], br.at[0, 0], other).wait_send()
        remote(sb.at[d], sb.at[d], dsm.at[d], br.at[0, 0], other).wait_send()
    for g in range(len(GROUPS)):
        core_copy(g).wait_send()
        plane_all(g).wait_send()
    store_h.wait()
    for i in range(4):
        for copy in store_rows(i):
            copy.wait()
    store_i.wait()


def finish(*refs):
    srcs, outs, held, sem = refs[:4], refs[4:8], refs[8:12], refs[12]
    parts = [(i, slice(j, j + 512)) for i in range(2, 4) for j in (0, 512)] + [(0, slice(0, TB)), (1, slice(0, 32))]
    loads = [pltpu.make_async_copy(srcs[i].at[r], held[i].at[r], sem.at[0, n]) for n, (i, r) in enumerate(parts)]
    stores = [pltpu.make_async_copy(held[i].at[r], outs[i].at[r], sem.at[1, n]) for n, (i, r) in enumerate(parts)]
    for load in loads:
        load.start()
    for load, store in zip(loads, stores):
        load.wait()
        store.start()
    for store in stores:
        store.wait()


def shards(tokens, gate_weight, up_weight, gate_mask, up_mask, grad_hidden):
    vmem = pl.BlockSpec(memory_space=pltpu.VMEM)
    hbm = pl.BlockSpec(memory_space=pl.ANY)
    dma = pltpu.SemaphoreType.DMA
    ng = len(GROUPS)
    shapes = (
        jax.ShapeDtypeStruct((TB, 512), BF16),
        jax.ShapeDtypeStruct((32, NZ * TB), BF16),
        jax.ShapeDtypeStruct((DB, 512), BF16),
        jax.ShapeDtypeStruct((DB, 512), BF16),
    )
    results = pl.pallas_call(
        kernel,
        out_shape=shapes,
        in_specs=[hbm, hbm, hbm, vmem, vmem, hbm],
        out_specs=(hbm,) * 4,
        scratch_shapes=[
            pltpu.VMEM((DB, 512), BF16),
            pltpu.VMEM((DB, 512), BF16),
            pltpu.VMEM((TB, 512), BF16),
            pltpu.VMEM((TB, 512), BF16),
            pltpu.VMEM((32, NZ * TB), BF16),
            pltpu.VMEM((DB, 512), BF16),
            pltpu.VMEM((DB, 512), BF16),
            pltpu.VMEM((DB, DB), BF16),
            pltpu.VMEM((2, 512, DB), BF16),
            pltpu.VMEM((16, 8, DB), F32),
            pltpu.VMEM((NZ, TB, DB), BF16),
            pltpu.VMEM((DB, NZ * TB), BF16),
            pltpu.VMEM((2, 14, TB, SW), BF16),
            pltpu.VMEM((2, 14, TB, SW), BF16),
            pltpu.VMEM((NZ, TB, DB), BF16),
            pltpu.VMEM((2, 16, 32, TB), BF16),
            pltpu.VMEM((3, 16, 32, 2 * TB), BF16),
            pltpu.VMEM((2, 16, 32, TB), BF16),
            pltpu.VMEM((3, 16, 32, 2 * TB), BF16),
            pltpu.VMEM((2, 16, 32, TB), BF16),
            pltpu.VMEM((3, 16, 32, 2 * TB), BF16),
            pltpu.VMEM((2, 15, 32, TB), BF16),
            pltpu.VMEM((3, 15, 32, 2 * TB), BF16),
            dma((3,)),
            dma((10,)),
            dma((1,)),
            dma((32,)),
            dma((2,)),
            dma((2, 14)),
            dma((2,)),
            dma((NZ, NS)),
            dma((ng,)),
            dma((ng,)),
            dma((ng,)),
            dma((ng,)),
        ],
        compiler_params=pltpu.CompilerParams(
            collective_id=0, has_side_effects=True, vmem_limit_bytes=56 * 1024 * 1024
        ),
    )(tokens, gate_weight, up_weight, gate_mask.T, up_mask.T, grad_hidden)
    hidden, git, og, ou = pl.pallas_call(
        finish,
        out_shape=shapes,
        in_specs=[hbm] * 4,
        out_specs=(hbm,) * 4,
        scratch_shapes=[pltpu.VMEM(shape.shape, BF16) for shape in shapes] + [dma((2, 6))],
        compiler_params=pltpu.CompilerParams(vmem_limit_bytes=56 * 1024 * 1024),
    )(*results)
    return hidden, git.T, og, ou


def solution(mesh):
    return jax.shard_map(
        shards,
        mesh=mesh,
        in_specs=(P("row", "col"),) * 6,
        out_specs=(P("row", "col"), P(None, ("row", "col")), P("row", "col"), P("row", "col")),
        check_vma=False,
    )
```

time: 426 us -> 86.2 us (0.20)
  waiting for transfers between devices: 361 us -> 0 us
  Pallas kernels: 0 us -> 85.3 us
  local copies, waits for them, and re-layouts: 22.3 us -> 0 us
  matrix products: 18.8 us -> 0 us
  between operations: 13.9 us -> 0.64 us
  other arithmetic: 4.76 us -> 0 us
  starting transfers between devices: 4.27 us -> 0 us
    all_gather x3 -> x0, waiting for transfers between devices: 289 us -> none  [the longest x1 173 us: shards(): lax.all_gather(local_pair, 'row', axis=0, tiled=True)]
    pallas_call x0 -> x2, Pallas kernels: none -> 85.3 us  [the longest x1 82.8 us: shards(): pl.pallas_call(kernel, out_shape=shapes, in_specs=[hbm, hbm, hbm, vmem, v...]
    unnamed x5 -> x0, waiting for transfers between devices: 72.6 us -> none
    dot_general x3 -> x0, matrix products: 18.8 us -> none  [the longest x1 8.7 us: shards(): jnp.dot(features, lax.all_gather(local_pair, 'row', axis=0, tiled=True),...]
    unnamed x22 -> x0, local copies, waits for them, and re-layouts: 12.6 us -> none
    gt x2 -> x0, local copies, waits for them, and re-layouts: 6.26 us -> none  [the longest x1 3.14 us: shards(): gate_keep = expand(gate_mask, block_size) > 0]
  transfers between devices with their start and end apart: 5 -> 0, of which waited for: 4 -> 0; matrix products, arithmetic and copies ran while one was open for 8% -> 0% of each run, Pallas kernels for 0% -> 0%
where the time goes in v2:
time: 86.2 us; the launch traced here: 85.9 us
  Pallas kernels  85.3 us (99%)
    pallas_call x1, Pallas kernels, shards(): pl.pallas_call(kernel, out_shape=shapes, in_specs=[hbm, hbm, hbm, vmem, v...  82.8 us
    pallas_call x1, Pallas kernels, shards(): pl.pallas_call(finish, out_shape=shapes, in_specs=[hbm] * 4, out_specs=(h...  2.51 us

profile of v2, /device:TPU:1, one launch (start us, length us, event | category | flops | bytes accessed | tf_op | source)
XLA Modules:
  0.0 85.9 jit_solution(2389522962180834203)
XLA Ops:
  0.6 82.8 %shard_map.93 = (bf16[128,512]{1,0:T(8,128)(2,1)}, bf16[32,1024]{1,0:T(8,128)(2,1)}, bf16[1024,512]{1,0:T(8,128)(2,1)}, bf16[1024,512]{1,0:T(8,128)(2,1)}) custom-call(bf16[128,256]{1,0:T(8,128)(2,1)} %tokens.1, bf16[1024,512]{1,0:T(8,128)(2,1)} %wg.1, bf16[1024,512]{1,0:T(8,128)(2,1)} %wu.1, s32[8,16]{1,0:T(8,128)} %bitcast.3, s32[8,16]{1,0:T(8,128)} %bitcast.4, ...), custom_call_target="tpu_custom_call" | custom-call | tf_op jit(solution)/shard_map/pallas_call | solution.py:364
  83.4 2.5 %shard_map.94 = (bf16[128,512]{1,0:T(8,128)(2,1)}, bf16[32,1024]{1,0:T(8,128)(2,1)}, bf16[1024,512]{1,0:T(8,128)(2,1)}, bf16[1024,512]{1,0:T(8,128)(2,1)}) custom-call(bf16[128,512]{1,0:T(8,128)(2,1)} %get-tuple-element.12.refs_0_, bf16[32,1024]{1,0:T(8,128)(2,1)} %get-tuple-element.13.refs_1_, bf16[1024,512]{1,0:T(8,128)(2,1)} %get-tuple-element.14.refs_2_, ...), custom_call_target="tpu_custom_call" | custom-call | tf_op jit(solution)/shard_map/pallas_call | solution.py:410

commit v3 on v2

--- a/solution.py
+++ b/solution.py
@@ -15,11 +15,14 @@
 DB = 1024
 SW = 256
 QW = 256
+HB = 64
+HALVES = (slice(0, HB), slice(HB, TB))
 OFFSET = (0, 1, -1, 2, -2, 3, -3, 4)
 GROUPS = ((0, 1), (1, 2), (3, 2), (5, 2), (7, 1))
-PLACE = ((2, 1), (1, 1), (3, 1), (2, 0), (0, 1), (1, 0), (3, 0), (0, 0))
+PLACE = ((2, 0), (1, 1), (2, 1), (0, 0), (3, 1), (3, 0), (0, 1), (1, 0))
 SLOT_AT = tuple(PLACE.index((i % 4, i // 4)) for i in range(8))
 REL = tuple(o % NZ for o in OFFSET)
+EARLY = (0, 0, 0, 0, 0, 1, 1, 1)
 SLOT_OF = tuple(REL.index(r) for r in range(NZ))
 
 
@@ -36,8 +39,8 @@
 def kernel(
     tokens, wg, wu, mg, mu, gh,
     hidden_out, git_out, og_out, ou_out,
-    wgv, wuv, ghv, hidden, git, og, ou, wp, we, mex, tv, tt, sb, rb, gv,
-    ps1, ps2, cr1, cr2, sx1, sx2, er1, er2,
+    mgv, muv, wgv, wuv, ghv, hidden, git, og, ou, wp, we, mex, tv, tt, sb, rb, gv,
+    ps1, ps2, cr1, cr2, ow1, ow2, sx1, sx2, er1, er2,
     lsem, osem, ts, tr, bs, br, dsm, dr, ecs, ecr, exs, exr,
 ):
     z = lax.axis_index("row")
@@ -55,8 +58,8 @@
         y_ = v_ + k * (u_ - v_)
         return (z, (x_ * 4 + y_) * 2 + k)
 
-    def tpiece(slot, q_):
-        return tv.at[slot, :, pl.ds(pl.multiple_of(q_ * QW, QW), QW)]
+    def tpiece(slot, q_, h):
+        return tv.at[slot, HALVES[h], pl.ds(pl.multiple_of(q_ * QW, QW), QW)]
 
     def piece(u_, v_):
         dx = (u_ + k * (v_ - u_) + 4 - x0) % 4
@@ -76,6 +79,10 @@
     s0, q0 = piece(u, v)
     frm = ((z + pick(REL, s0)) % NZ, 4 * z + q0)
 
+    load_mg = pltpu.make_async_copy(mg, mgv, lsem.at[3])
+    load_mu = pltpu.make_async_copy(mu, muv, lsem.at[4])
+    load_mg.start()
+    load_mu.start()
     load_g = pltpu.make_async_copy(wg, wgv, lsem.at[0])
     load_u = pltpu.make_async_copy(wu, wuv, lsem.at[1])
     load_h = pltpu.make_async_copy(gh, ghv, lsem.at[2])
@@ -89,10 +96,15 @@
         pl.semaphore_signal(barrier, inc=1, device_id=target, device_id_type=MESH)
     pl.semaphore_wait(barrier, 19)
 
-    remote(tokens, tpiece(slot_there, c % 4), ts.at[0], tr.at[slot_there * 4 + c % 4], to).start()
+    for h in range(2):
+        remote(
+            tokens.at[HALVES[h]], tpiece(slot_there, c % 4, h), ts.at[0], tr.at[slot_there * 4 + c % 4, h], to
+        ).start()
 
     lane = lax.broadcasted_iota(jnp.int32, (16, 128), 1) // 64
-    for which, mask in enumerate((mg, mu)):
+    load_mg.wait()
+    load_mu.wait()
+    for which, mask in enumerate((mgv, muv)):
         kept = jnp.where(mask[...] > 0, 1.0, 0.0).astype(F32).T
         for s in range(NS):
             kept_wide = jnp.where(lane == 0, kept[:, 2 * s : 2 * s + 1], kept[:, 2 * s + 1 : 2 * s + 2])
@@ -117,58 +129,70 @@
                 we[0, half, cols] = val[:32]
                 we[1, half, cols] = val[32:]
 
-    def send_piece(su, qu, target):
-        remote(tpiece(su, qu), tpiece(su, qu), ts.at[0], tr.at[su * 4 + qu], target).start()
-
-    def wait_piece(su, qu):
-        remote(tpiece(su, qu), tpiece(su, qu), ts.at[0], tr.at[su * 4 + qu], other).wait_recv()
-
-    wait_piece(s0, q0)
-    for d in (1, 3, 2):
-        send_piece(s0, q0, dev((u + d) % 4, v))
-    for d in (1, 3, 2):
-        send_piece(s0, q0, dev(u, (v + d) % 4))
-    for off in (0, 1, 3, 2):
-        line = (u0 + off) % 4
-
-        @pl.when(line != u)
-        def _(line=line):
-            su, qu = piece(line, v)
-            wait_piece(su, qu)
-            for d in (1, 3, 2):
-                send_piece(su, qu, dev(u, (v + d) % 4))
+    def send_piece(su, qu, h, target):
+        remote(tpiece(su, qu, h), tpiece(su, qu, h), ts.at[0], tr.at[su * 4 + qu, h], target).start()
+
+    def wait_piece(su, qu, h):
+        remote(tpiece(su, qu, h), tpiece(su, qu, h), ts.at[0], tr.at[su * 4 + qu, h], other).wait_recv()
+
+    def forward(line, early):
+        su, qu = piece(line, v)
+
+        @pl.when(jnp.logical_and(line != u, pick(EARLY, su) == early))
+        def _():
+            for h in range(2):
+                wait_piece(su, qu, h)
+                for d in (1, 3, 2):
+                    send_piece(su, qu, h, dev(u, (v + d) % 4))
+
+    for h in range(2):
+        wait_piece(s0, q0, h)
+        for d in (1, 3, 2):
+            send_piece(s0, q0, h, dev((u + d) % 4, v))
+    for early in (1, 0):
+
+        @pl.when(pick(EARLY, s0) == early)
+        def _():
+            for h in range(2):
+                for d in (1, 3, 2):
+                    send_piece(s0, q0, h, dev(u, (v + d) % 4))
+
+        for off in (0, 3, 1, 2):
+            forward((u0 + off) % 4, early)
 
     def swap(slot):
         for b in range(2):
             x_ = (x0 + PLACE[slot][0]) % 4
             y_ = (y0 + 2 * PLACE[slot][1] + b) % 4
             q_ = 2 * b + k
-
-            @pl.when(y_ + k * (x_ - y_) != v)
-            def _(q_=q_):
-                wait_piece(slot, q_)
-
-            send_piece(slot, q_, other)
+            for h in range(2):
+
+                @pl.when(y_ + k * (x_ - y_) != v)
+                def _(q_=q_, h=h):
+                    wait_piece(slot, q_, h)
+
+                send_piece(slot, q_, h, other)
 
     def ready(slot):
         for b in range(2):
-            wait_piece(slot, 2 * b + 1 - k)
+            for h in range(2):
+                wait_piece(slot, 2 * b + 1 - k, h)
 
     def transposed(slot, s):
         cols = slice(s * QW, s * QW + QW)
         tt[cols, slot * TB : slot * TB + TB] = tv[slot, :, cols].T
 
-    def b_copy(d, step, s):
-        i = s % 2 if step == 0 else 4 * step - 2 + s
-        return remote(sb.at[d, i], rb.at[d, i], bs.at[d], br.at[d, i], ring[d])
-
-    def b_in(d, step, s):
-        b_copy(d, step, s).wait_recv()
-        return rb[d, s % 2 if step == 0 else 4 * step - 2 + s].astype(F32)
-
-    def b_out(d, step, s, val):
-        sb[d, s % 2 if step == 0 else 4 * step - 2 + s] = val.astype(BF16)
-        b_copy(d, step, s).start()
+    def b_copy(d, step, s, h):
+        i = 4 * step + s
+        return remote(sb.at[d, i, HALVES[h]], rb.at[d, i, HALVES[h]], bs.at[d], br.at[d, i, h], ring[d])
+
+    def b_in(d, step, s, h):
+        b_copy(d, step, s, h).wait_recv()
+        return rb[d, 4 * step + s, HALVES[h], :].astype(F32)
+
+    def b_out(d, step, s, h, val):
+        sb[d, 4 * step + s, HALVES[h], :] = val.astype(BF16)
+        b_copy(d, step, s, h).start()
 
     def partial_sum(slot, count, s):
         rows = tv[slot : slot + count].reshape(count * TB, DB)
@@ -177,57 +201,74 @@
     for slot in (7, 5, 6):
         swap(slot)
     ready(7)
-    for s in (0, 2, 1, 3):
-        b_out(s // 2, 0, s, partial_sum(7, 1, s))
-    for slot in (3, 4):
-        swap(slot)
+    for s in range(NS):
+        val = partial_sum(7, 1, s)
+        for d in range(2):
+            b_out(d, 0, s, d, val[HALVES[d]])
     ready(5)
     ready(6)
-    for d, s in ((0, 2), (1, 0), (0, 3), (1, 1)):
-        b_out(d, 1, s, partial_sum(5 + d, 1, s))
-    for slot in (1, 2, 0):
-        swap(slot)
+
+    def first(s):
+        val = partial_sum(5, 2, s)
+        for d in range(2):
+            b_out(d, 1, s, 1 - d, val[d * TB + (1 - d) * HB : d * TB + (2 - d) * HB])
+        return [val[d * TB + d * HB : d * TB + (1 + d) * HB] for d in range(2)]
+
+    def second(s, rest):
+        for d in range(2):
+            b_out(d, 1, s, d, rest[d] + b_in(d, 0, s, d))
+
+    rests = [first(0), first(1)]
     for s in range(NS):
-        transposed(7, s)
-    for d, s in ((0, 0), (1, 2), (0, 1), (1, 3)):
-        val = partial_sum(5 + d, 1, s)
-        b_out(d, 1, s, val + b_in(d, 0, s))
+        for slot in (7, 5, 6):
+            transposed(slot, s)
+    second(0, rests[0])
+    rests.append(first(2))
+    second(1, rests[1])
+    rests.append(first(3))
+    second(2, rests[2])
+    second(3, rests[3])
+    swap(3)
+    swap(4)
     for step, slot in ((2, 3), (3, 1)):
         ready(slot)
         ready(slot + 1)
         for s in range(NS):
+            if step == 2 and s == 1:
+                for late in (1, 2, 0):
+                    swap(late)
             val = partial_sum(slot, 2, s)
+            for i in range(2):
+                for d in range(2):
+                    h = (1 - d + i) % 2
+                    b_out(d, step, s, h, val[d * TB + h * HB : d * TB + h * HB + HB] + b_in(d, step - 1, s, h))
+    ready(0)
+
+    def d_copy(dst, src, s, h, d):
+        cols = slice(s * SW, s * SW + SW)
+        there, here = gv.at[dst, HALVES[h], cols], gv.at[src, HALVES[h], cols]
+        return remote(here, there, dsm.at[d], dr.at[dst, s, h], ring[d])
+
+    def d_wait(slot, s, h):
+        d_copy(slot, slot, s, h, 0).wait_recv()
+
+    for s in range(NS):
+        own = partial_sum(0, 1, s)
+        hcols = slice(s * 128, s * 128 + 128)
+        for h in range(2):
+            val = own[HALVES[h]]
             for d in range(2):
-                b_out(d, step, s, val[d * TB : d * TB + TB] + b_in(d, step - 1, s))
-            transposed(slot, s)
-            transposed(slot + 1, s)
-            transposed(slot + 2, s)
-            if step == 2:
-                transposed(6, s)
-    ready(0)
-
-    def d_copy(dst, src, s, d):
-        cols = slice(s * SW, s * SW + SW)
-        return remote(gv.at[src, :, cols], gv.at[dst, :, cols], dsm.at[d], dr.at[dst, s], ring[d])
-
-    def d_wait(slot, s):
-        d_copy(slot, slot, s, 0).wait_recv()
-
-    for s in range(NS):
-        val = partial_sum(0, 1, s)
-        for d in range(2):
-            val = val + b_in(d, 3, s)
-        gate, up = val[:, :128], val[:, 128:]
-        hcols = slice(s * 128, s * 128 + 128)
-        up_grad = ghv[:, hcols].astype(F32)
-        sig = 1.0 / (1.0 + jnp.exp(-gate))
-        act = gate * sig
-        gv[0, :, s * SW : s * SW + 128] = (up_grad * up * sig * (1.0 + gate * (1.0 - sig))).astype(BF16)
-        gv[0, :, s * SW + 128 : s * SW + SW] = (up_grad * act).astype(BF16)
-        d_copy(2, 0, s, 0).start()
-        d_copy(1, 0, s, 1).start()
-        hidden[:, hcols] = (act * up).astype(BF16)
-        transposed(0, s)
+                val = val + b_in(d, 3, s, h)
+            gate, up = val[:, :128], val[:, 128:]
+            up_grad = ghv[HALVES[h], hcols].astype(F32)
+            sig = 1.0 / (1.0 + jnp.exp(-gate))
+            act = gate * sig
+            gate_grad = up_grad * up * sig * (1.0 + gate * (1.0 - sig))
+            gv[0, HALVES[h], s * SW : s * SW + 128] = gate_grad.astype(BF16)
+            gv[0, HALVES[h], s * SW + 128 : s * SW + SW] = (up_grad * act).astype(BF16)
+            d_copy(2, 0, s, h, 0).start()
+            d_copy(1, 0, s, h, 1).start()
+            hidden[HALVES[h], hcols] = (act * up).astype(BF16)
     store_h = pltpu.make_async_copy(hidden, hidden_out, osem.at[0])
     store_h.start()
 
@@ -247,11 +288,13 @@
         of_group(ps1, ps2, g)[...] = core_dot(g, 1 - k).astype(BF16)
         core_copy(g).start()
 
+    def own_dot(g):
+        of_group(ow1, ow2, g)[...] = core_dot(g, k)
+
     def e2(g):
-        val = core_dot(g, k)
         core_copy(g).wait_recv()
         sums = of_group(sx1, sx2, g)
-        sums[...] = (val + of_group(cr1, cr2, g)[...].astype(F32)).astype(BF16)
+        sums[...] = (of_group(ow1, ow2, g)[...] + of_group(cr1, cr2, g)[...].astype(F32)).astype(BF16)
         for d in range(1, 16):
             chip = ((x + d // 4) % 4) * 4 + (y + d % 4) % 4
             remote(sums.at[chip], of_group(er1, er2, g).at[d - 1], exs.at[g], exr.at[g], near[d]).start()
@@ -273,23 +316,34 @@
 
     for step in range(1, 4):
         for s in range(NS):
-            for d, slot in ((0, 2 * step), (1, 2 * step - 1)):
-                d_wait(slot, s)
-                if step < 3 or s // 2 == d:
-                    d_copy(min(slot + 2, 7), slot, s, d).start()
+            for h in range(2):
+                for d, slot in ((0, 2 * step), (1, 2 * step - 1)):
+                    d_wait(slot, s, h)
+                    if step < 3 or h == d:
+                        d_copy(min(slot + 2, 7), slot, s, h, d).start()
             if s == 0:
                 e1(step - 1)
+            elif s == 1:
+                own_dot(step - 1)
             elif s == 2:
                 e2(step - 1)
-            elif s == 3 and step > 1:
-                e3(step - 2)
-    d_wait(7, 0)
-    d_wait(7, 2)
-    e1(3)
-    d_wait(7, 1)
-    d_wait(7, 3)
+            else:
+                if step > 1:
+                    e3(step - 2)
+                for i in range(NS):
+                    for slot in ((3, 4), (1, 2), (0,))[step - 1]:
+                        transposed(slot, i)
+    for s in range(NS):
+        for h in range(2):
+            d_wait(7, s, h)
+        if s == 0:
+            e1(3)
+        elif s == 1:
+            own_dot(3)
+        elif s == 2:
+            e2(3)
     e1(4)
-    e2(3)
+    own_dot(4)
     e2(4)
 
     def store_rows(i):
@@ -322,10 +376,10 @@
     store_i = pltpu.make_async_copy(git, git_out, osem.at[1])
     store_i.start()
 
-    remote(tv, tv, ts.at[0], tr.at[0], other).wait_send()
+    remote(tv, tv, ts.at[0], tr.at[0, 0], other).wait_send()
     for d in range(2):
-        remote(sb.at[d], sb.at[d], bs.at[d], br.at[0, 0], other).wait_send()
-        remote(sb.at[d], sb.at[d], dsm.at[d], br.at[0, 0], other).wait_send()
+        remote(sb.at[d, 0:14], sb.at[d, 0:14], bs.at[d], br.at[0, 0, 0], other).wait_send()
+        remote(sb.at[d, 0:14], sb.at[d, 0:14], dsm.at[d], br.at[0, 0, 0], other).wait_send()
     for g in range(len(GROUPS)):
         core_copy(g).wait_send()
         plane_all(g).wait_send()
@@ -351,7 +405,6 @@
 
 
 def shards(tokens, gate_weight, up_weight, gate_mask, up_mask, grad_hidden):
-    vmem = pl.BlockSpec(memory_space=pltpu.VMEM)
     hbm = pl.BlockSpec(memory_space=pl.ANY)
     dma = pltpu.SemaphoreType.DMA
     ng = len(GROUPS)
@@ -364,9 +417,11 @@
     results = pl.pallas_call(
         kernel,
         out_shape=shapes,
-        in_specs=[hbm, hbm, hbm, vmem, vmem, hbm],
+        in_specs=[hbm] * 6,
         out_specs=(hbm,) * 4,
         scratch_shapes=[
+            pltpu.VMEM((8, 16), jnp.int32),
+            pltpu.VMEM((8, 16), jnp.int32),
             pltpu.VMEM((DB, 512), BF16),
             pltpu.VMEM((DB, 512), BF16),
             pltpu.VMEM((TB, 512), BF16),
@@ -379,25 +434,27 @@
             pltpu.VMEM((16, 8, DB), F32),
             pltpu.VMEM((NZ, TB, DB), BF16),
             pltpu.VMEM((DB, NZ * TB), BF16),
-            pltpu.VMEM((2, 14, TB, SW), BF16),
-            pltpu.VMEM((2, 14, TB, SW), BF16),
+            pltpu.VMEM((2, 16, TB, SW), BF16),
+            pltpu.VMEM((2, 16, TB, SW), BF16),
             pltpu.VMEM((NZ, TB, DB), BF16),
             pltpu.VMEM((2, 16, 32, TB), BF16),
             pltpu.VMEM((3, 16, 32, 2 * TB), BF16),
             pltpu.VMEM((2, 16, 32, TB), BF16),
             pltpu.VMEM((3, 16, 32, 2 * TB), BF16),
+            pltpu.VMEM((2, 16, 32, TB), F32),
+            pltpu.VMEM((3, 16, 32, 2 * TB), F32),
             pltpu.VMEM((2, 16, 32, TB), BF16),
             pltpu.VMEM((3, 16, 32, 2 * TB), BF16),
             pltpu.VMEM((2, 15, 32, TB), BF16),
             pltpu.VMEM((3, 15, 32, 2 * TB), BF16),
-            dma((3,)),
+            dma((5,)),
             dma((10,)),
             dma((1,)),
-            dma((32,)),
+            dma((32, 2)),
             dma((2,)),
-            dma((2, 14)),
+            dma((2, 16, 2)),
             dma((2,)),
-            dma((NZ, NS)),
+            dma((NZ, NS, 2)),
             dma((ng,)),
             dma((ng,)),
             dma((ng,)),

time: 86.2 us -> 83.7 us (0.971)
  Pallas kernels: 85.3 us -> 82.9 us
    pallas_call x1, Pallas kernels: 82.8 us -> 80.4 us  [shards(): pl.pallas_call(kernel, out_shape=shapes, in_specs=[hbm] * 6, out_specs=(h...]
where the time goes in v3:
time: 83.7 us; the launch traced here: 83.6 us
  Pallas kernels  82.9 us (99%)
    pallas_call x1, Pallas kernels, shards(): pl.pallas_call(kernel, out_shape=shapes, in_specs=[hbm] * 6, out_specs=(h...  80.4 us
    pallas_call x1, Pallas kernels, shards(): pl.pallas_call(finish, out_shape=shapes, in_specs=[hbm] * 4, out_specs=(h...  2.51 us

profile of v3, /device:TPU:1, one launch (start us, length us, event | category | flops | bytes accessed | tf_op | source)
XLA Modules:
  0.0 83.6 jit_solution(18261984426837724969)
XLA Ops:
  0.6 80.4 %shard_map.93 = (bf16[128,512]{1,0:T(8,128)(2,1)}, bf16[32,1024]{1,0:T(8,128)(2,1)}, bf16[1024,512]{1,0:T(8,128)(2,1)}, bf16[1024,512]{1,0:T(8,128)(2,1)}) custom-call(bf16[128,256]{1,0:T(8,128)(2,1)} %tokens.1, bf16[1024,512]{1,0:T(8,128)(2,1)} %wg.1, bf16[1024,512]{1,0:T(8,128)(2,1)} %wu.1, s32[8,16]{1,0:T(8,128)} %bitcast.3, s32[8,16]{1,0:T(8,128)} %bitcast.4, ...), custom_call_target="tpu_custom_call" | custom-call | tf_op jit(solution)/shard_map/pallas_call | solution.py:417
  81.0 2.5 %shard_map.94 = (bf16[128,512]{1,0:T(8,128)(2,1)}, bf16[32,1024]{1,0:T(8,128)(2,1)}, bf16[1024,512]{1,0:T(8,128)(2,1)}, bf16[1024,512]{1,0:T(8,128)(2,1)}) custom-call(bf16[128,512]{1,0:T(8,128)(2,1)} %get-tuple-element.12.refs_0_, bf16[32,1024]{1,0:T(8,128)(2,1)} %get-tuple-element.13.refs_1_, bf16[1024,512]{1,0:T(8,128)(2,1)} %get-tuple-element.14.refs_2_, ...), custom_call_target="tpu_custom_call" | custom-call | tf_op jit(solution)/shard_map/pallas_call | solution.py:467

commit v4 on v3

--- a/solution.py
+++ b/solution.py
@@ -24,6 +24,9 @@
 REL = tuple(o % NZ for o in OFFSET)
 EARLY = (0, 0, 0, 0, 0, 1, 1, 1)
 SLOT_OF = tuple(REL.index(r) for r in range(NZ))
+
+
+FAR_FIRST = sorted(range(1, 16), key=lambda d: -(min(d // 4, 4 - d // 4) + min(d % 4, 4 - d % 4)))
 
 
 def pick(table, i):
@@ -142,19 +145,19 @@
         def _():
             for h in range(2):
                 wait_piece(su, qu, h)
-                for d in (1, 3, 2):
+                for d in (2, 1, 3):
                     send_piece(su, qu, h, dev(u, (v + d) % 4))
 
     for h in range(2):
         wait_piece(s0, q0, h)
-        for d in (1, 3, 2):
+        for d in (2, 1, 3):
             send_piece(s0, q0, h, dev((u + d) % 4, v))
     for early in (1, 0):
 
         @pl.when(pick(EARLY, s0) == early)
         def _():
             for h in range(2):
-                for d in (1, 3, 2):
+                for d in (2, 1, 3):
                     send_piece(s0, q0, h, dev(u, (v + d) % 4))
 
         for off in (0, 3, 1, 2):
@@ -295,7 +298,7 @@
         core_copy(g).wait_recv()
         sums = of_group(sx1, sx2, g)
         sums[...] = (of_group(ow1, ow2, g)[...] + of_group(cr1, cr2, g)[...].astype(F32)).astype(BF16)
-        for d in range(1, 16):
+        for d in FAR_FIRST:
             chip = ((x + d // 4) % 4) * 4 + (y + d % 4) % 4
             remote(sums.at[chip], of_group(er1, er2, g).at[d - 1], exs.at[g], exr.at[g], near[d]).start()
 

time: 83.7 us -> 83.3 us (level)
  no operation moved by 1% of the time
where the time goes in v4:
time: 83.3 us; the launch traced here: 83.1 us
  Pallas kernels  82.5 us (99%)
    pallas_call x1, Pallas kernels, shards(): pl.pallas_call(kernel, out_shape=shapes, in_specs=[hbm] * 6, out_specs=(h...  80 us
    pallas_call x1, Pallas kernels, shards(): pl.pallas_call(finish, out_shape=shapes, in_specs=[hbm] * 4, out_specs=(h...  2.51 us

profile of v4, /device:TPU:1, one launch (start us, length us, event | category | flops | bytes accessed | tf_op | source)
XLA Modules:
  0.0 83.1 jit_solution(18135765050111749480)
XLA Ops:
  0.6 80.0 %shard_map.93 = (bf16[128,512]{1,0:T(8,128)(2,1)}, bf16[32,1024]{1,0:T(8,128)(2,1)}, bf16[1024,512]{1,0:T(8,128)(2,1)}, bf16[1024,512]{1,0:T(8,128)(2,1)}) custom-call(bf16[128,256]{1,0:T(8,128)(2,1)} %tokens.1, bf16[1024,512]{1,0:T(8,128)(2,1)} %wg.1, bf16[1024,512]{1,0:T(8,128)(2,1)} %wu.1, s32[8,16]{1,0:T(8,128)} %bitcast.3, s32[8,16]{1,0:T(8,128)} %bitcast.4, ...), custom_call_target="tpu_custom_call" | custom-call | tf_op jit(solution)/shard_map/pallas_call | solution.py:420
  80.6 2.5 %shard_map.94 = (bf16[128,512]{1,0:T(8,128)(2,1)}, bf16[32,1024]{1,0:T(8,128)(2,1)}, bf16[1024,512]{1,0:T(8,128)(2,1)}, bf16[1024,512]{1,0:T(8,128)(2,1)}) custom-call(bf16[128,512]{1,0:T(8,128)(2,1)} %get-tuple-element.12.refs_0_, bf16[32,1024]{1,0:T(8,128)(2,1)} %get-tuple-element.13.refs_1_, bf16[1024,512]{1,0:T(8,128)(2,1)} %get-tuple-element.14.refs_2_, ...), custom_call_target="tpu_custom_call" | custom-call | tf_op jit(solution)/shard_map/pallas_call | solution.py:470
